TPU v7x, 32 devices: a whole 2x2x4 slice. The times are simulated.
32 devices in a mesh: groups: 2 (over y), blk: 4 (over z), width: 4 (over x, core).
Axes of the slice: x: 2, y: 2, z: 4, core: 2. Of those that a mesh axis runs over, the one named last changes fastest.
Arguments:
- gate_pre: bfloat16 [448, 36864], P(('groups', 'width'), 'blk'), parts along dimension 0, may hold values from -6 to 6
- up_pre: bfloat16 [448, 36864], P(('groups', 'width'), 'blk'), parts along dimension 0, may hold values from -6 to 6
- down_weight: bfloat16 [36864, 9216], P('blk', 'width'), may hold values from -0.03125 to 0.03125
Outputs:
- mixed: bfloat16 [448, 9216], P(('groups', 'blk'), 'width'), parts along dimension 0
There are 2 independent parts, one for each index of `groups`. A program takes and returns all parts, laid end to end along the dimension named above; an argument that names none is the same for every part. Nothing has to cross between parts.
All inputs are finite; a program needn't handle non-finite values.
Results may differ from a plain program's by a relative error of at most 0.009.
Values may be sent and summed in bfloat16 or wider, within the bound.
A program may use at most 128 MiB of HBM per device.

v0:
```python
import jax
import jax.numpy as jnp
from jax import lax
from jax.sharding import PartitionSpec as P


def activation(gate_part, up_part):
    return (jax.nn.silu(gate_part.astype(jnp.float32)) * up_part.astype(jnp.float32)).astype(
        jnp.bfloat16
    )


def per_device(gate_pre, up_pre, down_weight):
    gate_all, up_all = (
        lax.all_gather(gate_pre, "width", axis=0, tiled=True),
        lax.all_gather(up_pre, "width", axis=0, tiled=True),
    )
    hidden = activation(gate_all, up_all)
    terms = jnp.dot(hidden, down_weight, preferred_element_type=jnp.float32)
    mixed = lax.psum_scatter(terms.astype(jnp.bfloat16), "blk", scatter_dimension=0, tiled=True)
    return mixed


def solution(mesh):
    return jax.shard_map(
        per_device,
        mesh=mesh,
        in_specs=(P(("groups", "width"), "blk"), P(("groups", "width"), "blk"), P("blk", "width")),
        out_specs=P(("groups", "blk"), "width"),
        check_vma=False,
    )
```

profile of v0, /device:TPU:0, one launch (start us, length us, event | category | flops | bytes accessed | tf_op | source)
XLA Modules:
  0.0 137.7 jit_solution(18320263169688309117)
XLA Ops:
  6.5 0.0 all-gather.3.cloned.1.call-start
  6.5 0.7 all-gather.3.cloned.1.call-update
  7.3 0.0 all-gather.5.cloned.1.call-start
  7.3 0.7 all-gather.5.cloned.1.call-update
  8.0 0.0 reduce-scatter.2.cloned.1.call-start
  8.1 37.7 %all-gather.3.cloned.1.call-done = bf16[224,9216]{1,0:T(8,128)(2,1)} async-done(((bf16[56,9216]{1,0:T(8,128)(2,1)}), bf16[224,9216]{1,0:T(8,128)(2,1)}) %all-gather.3.cloned.1.call-update) | async-done | bytes 4128784 | tf_op jit(solution)/shard_map/all_gather | solution.py:15
  45.8 35.7 %all-gather.5.cloned.1.call-done = bf16[224,9216]{1,0:T(8,128)(2,1)} async-done(((bf16[56,9216]{1,0:T(8,128)(2,1)}), bf16[224,9216]{1,0:T(8,128)(2,1)}) %all-gather.5.cloned.1.call-update) | async-done | bytes 4128784 | tf_op jit(solution)/shard_map/all_gather | solution.py:16
  81.5 22.4 %fusion.8 = bf16[224,2304]{1,0:T(8,128)(2,1)} fusion(bf16[9216,2304]{1,0:T(8,128)(2,1)} %param.5, bf16[224,9216]{1,0:T(8,128)(2,1)} %all-gather.5.cloned.1.call-done, bf16[224,9216]{1,0:T(8,128)(2,1)} %all-gather.3.cloned.1.call-done), kind=kOutput, calls=%fused_computation.9 | convolution fusion | flops 9529712640 | bytes 51757056 | tf_op jit(solution)/shard_map/dot_general | solution.py:19
  103.9 0.0 reduce-scatter.2.cloned.1.call-update
  103.9 27.2 %reduce-scatter.2.cloned.1.call-done = bf16[56,2304]{1,0:T(8,128)(2,1)} async-done(((bf16[224,2304]{1,0:T(8,128)(2,1)}), bf16[56,2304]{1,0:T(8,128)(2,1)}) %reduce-scatter.2.cloned.1.call-update) | async-done | bytes 258064 | tf_op jit(solution)/shard_map/reduce_scatter | solution.py:20
Async XLA Ops:
  6.5 39.2 %all-gather.3.cloned.1.call-start = ((), (), s32[]{:S(2)}) async-start(), calls=%async_computation.1 | async-start | bytes 5160960 | tf_op jit(solution)/shard_map/all_gather | solution.py:15
  7.3 74.2 %all-gather.5.cloned.1.call-start = ((), (), s32[]{:S(2)}) async-start(), calls=%async_computation.2 | async-start | bytes 5160960 | tf_op jit(solution)/shard_map/all_gather | solution.py:16
  8.0 123.1 %reduce-scatter.2.cloned.1.call-start = ((), (), s32[]{:S(2)}) async-start(), calls=%async_computation.3 | async-start | bytes 1290240 | tf_op jit(solution)/shard_map/reduce_scatter | solution.py:20
Sparse Core Ops, SparseCore 0:
  8.9 36.7 all-gather.2
  47.3 34.1 all-gather.4
  104.0 27.0 reduce-scatter.1
where the time goes:
time: 138 us
  waiting for transfers between devices  102 us (74%)
  matrix products  22.4 us (16%)
  between operations  13.1 us (9%)
    all_gather x1, waiting for transfers between devices, per_device(): lax.all_gather(gate_pre, 'width', axis=0, tiled=True)  37.7 us
    all_gather x1, waiting for transfers between devices, per_device(): lax.all_gather(up_pre, 'width', axis=0, tiled=True)  35.7 us
    reduce_scatter x1, waiting for transfers between devices, per_device(): lax.psum_scatter(terms.astype(jnp.bfloat16), 'blk', scatter_dimension=0,...  27.2 us
    dot_general x1, matrix products, per_device(): terms = jnp.dot(hidden, down_weight, preferred_element_type=jnp.float32)  22.4 us
  transfers between devices with their start and end apart: 3, of which 3 were waited for; matrix products, arithmetic and copies ran while one was open for 0% of the time, Pallas kernels for 0%

commit v1 on v0

v1 whole, which is shorter than its diff:
```python
import functools

import jax
import jax.numpy as jnp
from jax import lax
from jax.experimental import pallas as pl
from jax.experimental.pallas import tpu as pltpu
from jax.sharding import PartitionSpec as P

PIECES = 3
AHEAD = 2
HOP = 3
GAP = 3


def kernel(
    B, W, gate, up, weight, out,
    gate_v, up_v, w_v, hid_a, hid_b, acc_a, acc_b, tmp, send_buf, from_below, from_above,
    in_sem, w_sem, sib_send, sib_recv, x_send, x_recv, fwd_send, fwd_recv, rs_send, rs_below, rs_above,
):
    X = W // 2
    C, R, Kc = gate_v.shape
    q = B // W
    r = R // q
    Np = acc_a.shape[2]
    nA, nB = X + 1, X - 1
    z = lax.axis_index("blk")
    width = lax.axis_index("width")
    p, k = width // 2, width % 2
    sibling = {"width": p * 2 + 1 - k}
    first = (p * 2) // X

    def load(c):
        cols = pl.ds(pl.multiple_of(c * Kc, 128), Kc)
        return (
            pltpu.make_async_copy(gate.at[:, cols], gate_v.at[c], in_sem.at[0, c]),
            pltpu.make_async_copy(up.at[:, cols], up_v.at[c], in_sem.at[1, c]),
        )

    def load_weight(c):
        rows = pl.ds(pl.multiple_of(c * Kc, 128), Kc)
        return pltpu.make_async_copy(weight.at[rows, :], w_v.at[c], w_sem.at[c])

    def to_sibling(c):
        return pltpu.make_async_remote_copy(
            hid_a.at[c, k], hid_a.at[c, k], sib_send.at[c], sib_recv.at[c],
            device_id=sibling, device_id_type=pl.DeviceIdType.MESH,
        )

    def from_sibling(c):
        return pltpu.make_async_remote_copy(
            hid_a.at[c, 1 - k], hid_a.at[c, 1 - k], sib_send.at[c], sib_recv.at[c],
            device_id=sibling, device_id_type=pl.DeviceIdType.MESH,
        )

    def across(phase, o, c):
        peer = lax.rem(p + o, X) * 2 + k
        src = hid_a.at[c, first] if phase == 0 else hid_a.at[c, 1 - first]
        dst = hid_a.at[c, 1 + o] if phase == 0 else hid_b.at[c, o - 1]
        return pltpu.make_async_remote_copy(
            src, dst, x_send.at[phase, o - 1, c], x_recv.at[phase, o - 1, c],
            device_id={"width": peer}, device_id_type=pl.DeviceIdType.MESH,
        )

    def forward(phase, o, c):
        ref = hid_a.at[c, 1 + o] if phase == 0 else hid_b.at[c, o - 1]
        return pltpu.make_async_remote_copy(
            ref, ref, fwd_send.at[phase, o - 1, c], fwd_recv.at[phase, o - 1, c],
            device_id=sibling, device_id_type=pl.DeviceIdType.MESH,
        )

    def mine(c):
        return lax.rem(c, 2) == k

    def send_across(phase, c):
        for o in range(1, X):
            across(phase, o, c).start()

    def service(phase, c):
        @pl.when(mine(c))
        def _():
            for o in range(1, X):
                across(phase, o, c).wait_recv()
                forward(phase, o, c).start()

    def arrived(phase, c):
        @pl.when(jnp.logical_not(mine(c)))
        def _():
            for o in range(1, X):
                forward(phase, o, c).wait_recv()

    def loop(n, body):
        lax.fori_loop(0, n, lambda i, _: (body(i), 0)[1], 0)

    def start_loads(c):
        a, b = load(c)
        a.start()
        b.start()

    loop(C, start_loads)
    loop(C, lambda c: load_weight(c).start())

    barrier = pltpu.get_barrier_semaphore()

    def greet(device):
        pl.semaphore_signal(barrier, inc=1, device_id=device, device_id_type=pl.DeviceIdType.MESH)

    greet(sibling)
    for o in range(1, X):
        greet({"width": lax.rem(p + o, X) * 2 + k})
    pl.when(z > 0)(lambda: greet({"blk": z - 1}))
    pl.when(z < B - 1)(lambda: greet({"blk": z + 1}))
    pl.semaphore_wait(barrier, X + jnp.minimum(z, 1) + jnp.minimum(B - 1 - z, 1))

    def activate(c):
        a, b = load(c)
        a.wait()
        b.wait()
        v = gate_v[c].astype(jnp.float32)
        h = v / (1.0 + jnp.exp(-v)) * up_v[c].astype(jnp.float32)
        hid_a[c, k] = h.astype(jnp.bfloat16)
        pl.when(jnp.logical_and(mine(c), first == k))(lambda: send_across(0, c))
        to_sibling(c).start()

    loop(C, activate)

    def exchange(c):
        from_sibling(c).wait_recv()
        pl.when(jnp.logical_and(mine(c), first != k))(lambda: send_across(0, c))

    loop(C, exchange)

    def multiply(hid, acc, c, pieces):
        n_slots = hid.shape[1]
        lhs = hid[c].reshape(n_slots * R, Kc)
        for n in pieces:
            acc[n] += jnp.dot(
                lhs, w_v[c, :, n * Np : (n + 1) * Np], preferred_element_type=jnp.float32
            )

    acc_a[...] = jnp.zeros_like(acc_a)
    acc_b[...] = jnp.zeros_like(acc_b)
    ahead = min(AHEAD, C)
    for c in range(ahead):
        service(0, c)

    def step_a(c):
        pl.when(c + ahead < C)(lambda: service(0, c + ahead))
        pl.when(mine(c))(lambda: send_across(1, c))
        load_weight(c).wait()
        arrived(0, c)
        multiply(hid_a, acc_a, c, range(PIECES))

    loop(C, step_a)

    def hop(acc, idx, step, j, n):
        rows = pl.ds(pl.multiple_of(idx * r, 8), r)
        below = pltpu.make_async_remote_copy(
            send_buf.at[step], from_below.at[step], rs_send.at[step], rs_below.at[step],
            device_id={"blk": jnp.minimum(z + 1, B - 1)}, device_id_type=pl.DeviceIdType.MESH,
        )
        above = pltpu.make_async_remote_copy(
            send_buf.at[step], from_above.at[step], rs_send.at[step], rs_above.at[step],
            device_id={"blk": jnp.maximum(z - 1, 0)}, device_id_type=pl.DeviceIdType.MESH,
        )
        tmp[...] = acc[n, rows, :]

        @pl.when(jnp.logical_and(z <= j, z > 0))
        def _():
            below.wait_recv()
            tmp[...] += from_below[step].astype(jnp.float32)

        @pl.when(jnp.logical_and(z >= j, z < B - 1))
        def _():
            above.wait_recv()
            tmp[...] += from_above[step].astype(jnp.float32)

        @pl.when(z != j)
        def _():
            send_buf[step] = tmp[...].astype(jnp.bfloat16)

        pl.when(z < j)(lambda: below.start())
        pl.when(z > j)(lambda: above.start())

        @pl.when(z == j)
        def _():
            out[:, pl.ds(pl.multiple_of(n * Np, 128), Np)] = tmp[...].astype(jnp.bfloat16)

    def slab_of(slot):
        o = jnp.where(slot < nA, slot - 1, slot - nA + 1)
        chip = lax.rem(p - o + 2 * X, X)
        lead = (chip * 2) // X
        remote = chip * 2 + jnp.where(slot < nA, lead, 1 - lead)
        return jnp.where(slot < 2, p * 2 + slot, remote)

    def distance(j):
        return jnp.where(z < j, z, jnp.where(z > j, B - 1 - z, jnp.maximum(z, B - 1 - z)))

    def reduce_a(t):
        def one(idx):
            j = slab_of(idx // q) * q + lax.rem(idx, q)
            rest = t - distance(j) * HOP
            n = rest // GAP

            @pl.when(jnp.logical_and(rest >= 0, jnp.logical_and(rest == n * GAP, n < PIECES)))
            def _():
                hop(acc_a, idx, idx * PIECES + n, j, n)

        loop(nA * q, one)

    def reduce_b(n, ends):
        def one(idx):
            j = slab_of(nA + idx // q) * q + lax.rem(idx, q)
            end = jnp.logical_or(
                jnp.logical_and(z < j, z == 0), jnp.logical_and(z > j, z == B - 1)
            )

            @pl.when(end == ends)
            def _():
                hop(acc_b, idx, (nA * q + idx) * PIECES + n, j, n)

        loop(nB * q, one)

    for c in range(ahead):
        service(1, c)

    def step_b(c):
        pl.when(c + ahead < C)(lambda: service(1, c + ahead))
        reduce_a(c)
        arrived(1, c)
        multiply(hid_b, acc_b, c, range(PIECES))

    loop(C - 1, step_b)
    arrived(1, C - 1)
    for n in range(PIECES):
        multiply(hid_b, acc_b, C - 1, [n])
        reduce_b(n, True)
    last = (B - 1) * HOP + (PIECES - 1) * GAP
    loop(max(last + 1 - (C - 1), 0), lambda t: reduce_a(t + C - 1))
    loop(PIECES, lambda n: reduce_b(n, False))

    def finish(c):
        to_sibling(c).wait_send()

        @pl.when(mine(c))
        def _():
            for phase in range(2):
                for o in range(1, X):
                    across(phase, o, c).wait_send()
                    forward(phase, o, c).wait_send()

    loop(C, finish)

    def finish_sum(step):
        slot = step // (PIECES * q)
        j = slab_of(slot) * q + lax.rem(step // PIECES, q)

        @pl.when(z != j)
        def _():
            pltpu.make_async_remote_copy(
                send_buf.at[step], from_below.at[step], rs_send.at[step], rs_below.at[step],
                device_id={"blk": jnp.where(z < j, z + 1, z - 1)},
                device_id_type=pl.DeviceIdType.MESH,
            ).wait_send()

    loop(W * q * PIECES, finish_sum)


def per_device(B, W, gate_pre, up_pre, down_weight):
    R, K = gate_pre.shape
    N = down_weight.shape[1]
    X = W // 2
    Kc = next(s for s in (768, 384, 256, 128) if K % s == 0)
    C = K // Kc
    r = R * W // B
    Np = N // PIECES
    steps = B * PIECES
    bf16, f32 = jnp.bfloat16, jnp.float32
    dma = pltpu.SemaphoreType.DMA
    return pl.pallas_call(
        functools.partial(kernel, B, W),
        out_shape=jax.ShapeDtypeStruct((r, N), bf16),
        in_specs=[pl.BlockSpec(memory_space=pl.ANY)] * 3,
        out_specs=pl.BlockSpec(memory_space=pltpu.VMEM),
        scratch_shapes=[
            pltpu.VMEM((C, R, Kc), bf16),
            pltpu.VMEM((C, R, Kc), bf16),
            pltpu.VMEM((C, Kc, N), bf16),
            pltpu.VMEM((C, X + 1, R, Kc), bf16),
            pltpu.VMEM((C, X - 1, R, Kc), bf16),
            pltpu.VMEM((PIECES, (X + 1) * R, Np), f32),
            pltpu.VMEM((PIECES, (X - 1) * R, Np), f32),
            pltpu.VMEM((r, Np), f32),
            pltpu.VMEM((steps, r, Np), bf16),
            pltpu.VMEM((steps, r, Np), bf16),
            pltpu.VMEM((steps, r, Np), bf16),
            dma((2, C)),
            dma((C,)),
            dma((C,)),
            dma((C,)),
            dma((2, X - 1, C)),
            dma((2, X - 1, C)),
            dma((2, X - 1, C)),
            dma((2, X - 1, C)),
            dma((steps,)),
            dma((steps,)),
            dma((steps,)),
        ],
        compiler_params=pltpu.CompilerParams(
            collective_id=0, has_side_effects=True, vmem_limit_bytes=62 * 1024 * 1024
        ),
    )(gate_pre, up_pre, down_weight)


def solution(mesh):
    return jax.shard_map(
        functools.partial(per_device, mesh.shape["blk"], mesh.shape["width"]),
        mesh=mesh,
        in_specs=(P(("groups", "width"), "blk"), P(("groups", "width"), "blk"), P("blk", "width")),
        out_specs=P(("groups", "blk"), "width"),
        check_vma=False,
    )
```

time: 138 us -> 50.4 us (0.37)
  the two profiles are of different devices: /device:TPU:0 before, /device:TPU:16 now
where the time goes in v1:
time: 50.4 us; the launch traced here: 50.3 us
  Pallas kernels  48.6 us (96%)
  local copies, waits for them, and re-layouts  1.66 us (3%)
    pallas_call x1, Pallas kernels, per_device(): pl.pallas_call(functools.partial(kernel, B, W), out_shape=jax.ShapeDtypeS...  48.6 us
    unnamed x1, local copies, waits for them, and re-layouts  1.66 us

profile of v1, /device:TPU:16, one launch (start us, length us, event | category | flops | bytes accessed | tf_op | source)
XLA Modules:
  0.0 50.3 jit_solution(15690410049942171082)
XLA Ops:
  0.0 48.6 %shard_map.37 = bf16[56,2304]{1,0:T(8,128)(2,1)} custom-call(bf16[56,9216]{1,0:T(8,128)(2,1)} %gate.1, bf16[56,9216]{1,0:T(8,128)(2,1)} %up.1, bf16[9216,2304]{1,0:T(8,128)(2,1)} %weight.1), custom_call_target="tpu_custom_call" | custom-call | tf_op jit(solution)/shard_map/pallas_call | solution.py:280
  48.6 1.7 %copy.5 = bf16[56,2304]{1,0:T(8,128)(2,1)} copy(bf16[56,2304]{1,0:T(8,128)(2,1)} %shard_map.37) | data formatting | bytes 516096

commit v2 on v1

--- a/solution.py
+++ b/solution.py
@@ -8,9 +8,9 @@
 from jax.sharding import PartitionSpec as P
 
 PIECES = 3
-AHEAD = 2
-HOP = 3
-GAP = 3
+AHEAD = 1
+HOP = 2
+GAP = 1
 
 
 def kernel(
@@ -110,6 +110,8 @@
         greet({"width": lax.rem(p + o, X) * 2 + k})
     pl.when(z > 0)(lambda: greet({"blk": z - 1}))
     pl.when(z < B - 1)(lambda: greet({"blk": z + 1}))
+    acc_a[...] = jnp.zeros_like(acc_a)
+    acc_b[...] = jnp.zeros_like(acc_b)
     pl.semaphore_wait(barrier, X + jnp.minimum(z, 1) + jnp.minimum(B - 1 - z, 1))
 
     def activate(c):
@@ -138,8 +140,6 @@
                 lhs, w_v[c, :, n * Np : (n + 1) * Np], preferred_element_type=jnp.float32
             )
 
-    acc_a[...] = jnp.zeros_like(acc_a)
-    acc_b[...] = jnp.zeros_like(acc_b)
     ahead = min(AHEAD, C)
     for c in range(ahead):
         service(0, c)
@@ -270,7 +270,7 @@
     R, K = gate_pre.shape
     N = down_weight.shape[1]
     X = W // 2
-    Kc = next(s for s in (768, 384, 256, 128) if K % s == 0)
+    Kc = next(s for s in (1536, 384, 256, 128) if K % s == 0)
     C = K // Kc
     r = R * W // B
     Np = N // PIECES

time: 50.4 us -> 49.1 us (0.974)
  Pallas kernels: 48.6 us -> 47.3 us
    pallas_call x1, Pallas kernels: 48.6 us -> 47.3 us  [per_device(): pl.pallas_call(functools.partial(kernel, B, W), out_shape=jax.ShapeDtypeS...]
where the time goes in v2:
time: 49.1 us; the launch traced here: 49 us
  Pallas kernels  47.3 us (96%)
  local copies, waits for them, and re-layouts  1.66 us (3%)
    pallas_call x1, Pallas kernels, per_device(): pl.pallas_call(functools.partial(kernel, B, W), out_shape=jax.ShapeDtypeS...  47.3 us
    unnamed x1, local copies, waits for them, and re-layouts  1.66 us

profile of v2, /device:TPU:16, one launch (start us, length us, event | category | flops | bytes accessed | tf_op | source)
XLA Modules:
  0.0 49.0 jit_solution(17967766801526746760)
XLA Ops:
  0.0 47.3 %shard_map.37 = bf16[56,2304]{1,0:T(8,128)(2,1)} custom-call(bf16[56,9216]{1,0:T(8,128)(2,1)} %gate.1, bf16[56,9216]{1,0:T(8,128)(2,1)} %up.1, bf16[9216,2304]{1,0:T(8,128)(2,1)} %weight.1), custom_call_target="tpu_custom_call" | custom-call | tf_op jit(solution)/shard_map/pallas_call | solution.py:280
  47.3 1.7 %copy.5 = bf16[56,2304]{1,0:T(8,128)(2,1)} copy(bf16[56,2304]{1,0:T(8,128)(2,1)} %shard_map.37) | data formatting | bytes 516096
